TPU v7x, 32 devices: a whole 2x2x4 slice. The times are simulated.
32 devices in a mesh: shell: 2 (over y), row: 4 (over x, core), col: 4 (over z).
Axes of the slice: x: 2, y: 2, z: 4, core: 2. Of those that a mesh axis runs over, the one named last changes fastest.
Arguments:
- left_basis: bfloat16 [2, 1024, 1536], P(None, 'row', 'shell'), may hold values from -6 to 6
- right_basis: bfloat16 [2, 1536, 2048], P(None, 'shell', 'col'), may hold values from -0.15625 to 0.15625
- point_weight: float32 [1536], P('shell'), may hold values from 0.3 to 3
- shell_index: int32 [1536], P('shell'), may hold values from 0 to 11
- green_table: float32 [12, 2], replicated, may hold values from -4 to 4
- pivot_rows: int32 [512], replicated, may hold values from 0 to 1023, as said below
- diag_inverse: bfloat16 [2, 512, 512], replicated, may hold values from -0.005859375 to 0.005859375
Outputs:
- factored: float32 [2, 4, 2, 128, 2048], P(None, 'row', 'shell', None, 'col')
Inputs may be any that keep to these rules, and one draw needn't show every extreme that they name: `pivot_rows`: 512 distinct matrix rows.
All inputs are finite; a program needn't handle non-finite values.
Results may differ from a plain program's by a relative error of at most 0.0056.
Values may be sent and summed in bfloat16 or wider, within the bound.
A program may use at most 128 MiB of HBM per device.

v0:
```python
import jax
import jax.numpy as jnp
from jax import lax
from jax.sharding import PartitionSpec as P


def broadcast(block, axis, source):
    block = jnp.where(lax.axis_index(axis) == source, block, jnp.zeros_like(block))
    return lax.psum(block, axis)


def complex_block(real_part, imag_part):
    upper_half = jnp.concatenate([real_part, imag_part], axis=1)
    lower_half = jnp.concatenate([-imag_part, real_part], axis=1)
    return jnp.concatenate([upper_half, lower_half], axis=0)


def weigh_points(right_basis, point_weight, shell_index, green_table):
    shells_count = green_table.shape[0]
    matches = shell_index[:, None] == jnp.arange(shells_count, dtype=jnp.int32)[None, :]
    green_real = jnp.sum(jnp.where(matches, green_table[None, :, 0], 0.0), axis=1)
    green_imag = jnp.sum(jnp.where(matches, green_table[None, :, 1], 0.0), axis=1)
    weight_real = point_weight * green_real
    weight_imag = point_weight * green_imag
    basis_real = right_basis[0].astype(jnp.float32)
    basis_imag = right_basis[1].astype(jnp.float32)
    weighted_real = (weight_real[:, None] * basis_real - weight_imag[:, None] * basis_imag).astype(
        jnp.bfloat16
    )
    weighted_imag = (weight_real[:, None] * basis_imag + weight_imag[:, None] * basis_real).astype(
        jnp.bfloat16
    )
    return (weighted_real, weighted_imag)


def reduce_tiles(term_rows, owned_rows):
    return lax.psum_scatter(
        term_rows(jnp.int32(0), owned_rows * lax.axis_size("shell")),
        "shell",
        scatter_dimension=0,
        tiled=True,
    )


def pick_rows(matrix_rows, pivot_rows, row_base):
    held_rows = matrix_rows.shape[0]
    local_index = pivot_rows - row_base
    inside = (local_index >= 0) & (local_index < held_rows)
    picked = jnp.take(matrix_rows, jnp.clip(local_index, 0, held_rows - 1), axis=0)
    return jnp.where(inside[:, None], picked, 0.0)


def select_pivots(coupling, pivot_rows, row_base):
    picked = pick_rows(coupling, pivot_rows, row_base).astype(jnp.bfloat16)
    return lax.psum(picked, ("shell", "row")).astype(jnp.float32).astype(jnp.bfloat16)


def body(left_basis, right_basis, point_weight, shell_index, green_table, pivot_rows, diag_inverse):
    shells = lax.axis_size("shell")
    owned_rows = left_basis.shape[1] // shells
    panel_width = right_basis.shape[2]
    weighted_real, weighted_imag = weigh_points(right_basis, point_weight, shell_index, green_table)
    grid_row = lax.axis_index("row")
    shell_rank = lax.axis_index("shell")
    row_base = (grid_row * shells + shell_rank) * owned_rows
    left_stack = jnp.concatenate([left_basis[0], left_basis[1]], axis=1)
    right_stack = complex_block(weighted_real, weighted_imag)

    def from_bases(first_row, row_count):
        return jnp.dot(left_stack, right_stack, preferred_element_type=jnp.float32)

    coupling = reduce_tiles(from_bases, owned_rows)
    pivot_sum = select_pivots(coupling, pivot_rows, row_base)
    panel_real = coupling[:, :panel_width]
    panel_imag = coupling[:, panel_width:]
    inverse_real = diag_inverse[0].astype(jnp.float32)
    inverse_imag = diag_inverse[1].astype(jnp.float32)
    highest = lax.Precision.HIGHEST
    mult_real = (
        jnp.dot(panel_real, inverse_real, precision=highest, preferred_element_type=jnp.float32)
        - jnp.dot(panel_imag, inverse_imag, precision=highest, preferred_element_type=jnp.float32)
    ).astype(jnp.bfloat16)
    mult_imag = (
        jnp.dot(panel_real, inverse_imag, precision=highest, preferred_element_type=jnp.float32)
        + jnp.dot(panel_imag, inverse_real, precision=highest, preferred_element_type=jnp.float32)
    ).astype(jnp.bfloat16)
    multipliers = jnp.concatenate([mult_real, mult_imag], axis=1)
    multipliers = broadcast(multipliers, "col", 0)
    pivot_block = complex_block(pivot_sum[:, :panel_width], pivot_sum[:, panel_width:])
    update = jnp.dot(multipliers, pivot_block, preferred_element_type=jnp.float32)
    updated = coupling - update
    return jnp.stack([updated[:, :panel_width], updated[:, panel_width:]]).reshape(
        2, 1, 1, owned_rows, panel_width
    )


def solution(mesh):
    return jax.shard_map(
        body,
        mesh=mesh,
        in_specs=(
            P(None, "row", "shell"),
            P(None, "shell", "col"),
            P("shell"),
            P("shell"),
            P(),
            P(),
            P(),
        ),
        out_specs=P(None, "row", "shell", None, "col"),
        check_vma=False,
    )
```

profile of v0, /device:TPU:1, one launch (start us, length us, event | category | flops | bytes accessed | tf_op | source)
XLA Modules:
  0.0 142.7 jit_solution(1994060089724896081)
XLA Ops:
  6.5 0.0 reduce-scatter.2.cloned.1.call-start
  6.5 0.8 slice_bitcast_fusion.4
  7.3 0.8 select_reduce_fusion.1
  8.1 0.7 fusion.44
  8.8 0.0 copy-start.1
  8.8 1.9 %fusion.42 = (bf16[768,512]{1,0:T(8,128)(2,1)S(1)}, bf16[768,512]{1,0:T(8,128)(2,1)S(1)}) fusion(bf16[2,768,512]{2,1,0:T(8,128)(2,1)} %param.8, f32[768]{0:T(1024)S(1)} %get-tuple-element.18, f32[768]{0:T(1024)S(1)} %get-tuple-element.17), kind=kLoop, calls=%fused_computation.64 | loop fusion | flops 2752512 | bytes 3151872 | tf_op jit(solution)/shard_map/neg | solution.py:14
  10.7 0.0 copy-done.1
  10.7 0.0 copy-start.4
  10.7 0.4 fusion.15
  11.1 0.7 copy-done.4
  11.8 0.1 slice_bitcast_fusion.1
  11.9 0.0 copy-start.5
  11.9 1.9 %fusion = f32[256,1024]{1,0:T(8,128)} fusion(bf16[768,512]{1,0:T(8,128)(2,1)S(1)} %fusion.15, bf16[768,512]{1,0:T(8,128)(2,1)S(1)} %get-tuple-element.9, bf16[768,512]{1,0:T(8,128)(2,1)S(1)} %get-tuple-element.10, bf16[256,768]{1,0:T(8,128)(2,1)S(1)} %get-tuple-element.14, bf16[256,768]{1,0:T(8,128)(2,1)S(1)} %get-tuple-element.13), kind=kOutput, calls=%fused_computation.1 | convolution fusion | flops 819462144 | bytes 4194304 | tf_op jit(solution)/shard_map/dot_general | solution.py:70
  13.8 0.0 reduce-scatter.2.cloned.1.call-update
  13.9 0.0 all-reduce.5.cloned.1.call-start
  13.9 0.0 copy-done.5
  14.0 22.4 %reduce-scatter.2.cloned.1.call-done = f32[128,1024]{1,0:T(8,128)} async-done(((f32[256,1024]{1,0:T(8,128)}), f32[128,1024]{1,0:T(8,128)}) %reduce-scatter.2.cloned.1.call-update) | async-done | bytes 524304 | tf_op jit(solution)/shard_map/reduce_scatter | solution.py:37
  36.4 3.8 %gather_fusion = bf16[512,1024]{1,0:T(8,128)(2,1)S(1)} fusion(f32[128,1024]{1,0:T(8,128)} %reduce-scatter.2.cloned.1.call-done, s32[1024]{0:T(1024)S(1)} %pad_clamp_fusion), kind=kCustom, calls=%fused_computation | custom fusion | bytes 2099200 | tf_op jit(solution)/shard_map/jit(_take)/gather | solution.py:49
  40.2 0.0 copy-start
  40.2 0.0 copy-start.2
  40.2 1.4 select_convert_fusion
  41.6 0.0 all-reduce.5.cloned.1.call-update
  41.6 0.0 all-reduce.3.cloned.1.call-start
  41.6 0.0 copy-done
  41.7 0.2 copy-done.2
  41.8 0.4 fusion.30
  42.2 0.4 fusion.21
  42.6 0.4 fusion.26
  43.0 0.4 fusion.22
  43.4 0.8 maximum_select_fusion
  44.1 0.0 all-reduce.3.cloned.1.call-update
  44.2 53.2 %all-reduce.5.cloned.1.call-done = bf16[512,1024]{1,0:T(8,128)(2,1)} async-done(((bf16[512,1024]{1,0:T(8,128)(2,1)}), bf16[512,1024]{1,0:T(8,128)(2,1)}) %all-reduce.5.cloned.1.call-update) | async-done | bytes 1048592 | tf_op jit(solution)/shard_map/psum | solution.py:55
  97.3 0.0 copy-start.3
  97.3 1.4 slice_negate_fusion
  98.7 35.2 %all-reduce.3.cloned.1.call-done = bf16[128,1024]{1,0:T(8,128)(2,1)} async-done(((bf16[128,1024]{1,0:T(8,128)(2,1)}), bf16[128,1024]{1,0:T(8,128)(2,1)}) %all-reduce.3.cloned.1.call-update) | async-done | bytes 262160 | tf_op jit(solution)/shard_map/psum | solution.py:9
  133.8 0.0 copy-done.3
  133.9 1.4 fusion.18
  135.3 0.8 maximum_bitcast_fusion
  (3 shorter events, 0.1 us)
Async XLA Ops:
  6.5 29.9 %reduce-scatter.2.cloned.1.call-start = ((), (), s32[]{:S(2)}) async-start(), calls=%async_computation.1 | async-start | bytes 1572864 | tf_op jit(solution)/shard_map/reduce_scatter | solution.py:37
  8.8 1.9 %copy-start.1 = (bf16[2,768,512]{2,1,0:T(8,128)(2,1)S(1)}, bf16[2,768,512]{2,1,0:T(8,128)(2,1)}, u32[]{:S(2)}) copy-start(bf16[2,768,512]{2,1,0:T(8,128)(2,1)} %param.8) | copy-start | bytes 4718596
  10.7 1.1 copy-start.4
  11.9 2.0 %copy-start.5 = (s32[512]{0:T(512)S(1)}, s32[512]{0:T(512)}, u32[]{:S(2)}) copy-start(s32[512]{0:T(512)} %param.12) | copy-start | bytes 6148
  13.9 83.5 %all-reduce.5.cloned.1.call-start = ((), (), s32[]{:S(2)}) async-start(), calls=%async_computation.3 | async-start | bytes 2097152 | tf_op jit(solution)/shard_map/psum | solution.py:55
  40.2 1.5 %copy-start = (f32[128,1024]{1,0:T(8,128)S(1)}, f32[128,1024]{1,0:T(8,128)}, u32[]{:S(2)}) copy-start(f32[128,1024]{1,0:T(8,128)} %reduce-scatter.2.cloned.1.call-done) | copy-start | bytes 1572868
  40.2 1.6 %copy-start.2 = (bf16[2,512,512]{2,1,0:T(8,128)(2,1)S(1)}, bf16[2,512,512]{2,1,0:T(8,128)(2,1)}, u32[]{:S(2)}) copy-start(bf16[2,512,512]{2,1,0:T(8,128)(2,1)} %param.13) | copy-start | bytes 3145732
  41.6 92.3 %all-reduce.3.cloned.1.call-start = ((), (), s32[]{:S(2)}) async-start(), calls=%async_computation.2 | async-start | bytes 524288 | tf_op jit(solution)/shard_map/psum | solution.py:9
  97.3 36.5 %copy-start.3 = (bf16[512,1024]{1,0:T(8,128)(2,1)S(1)}, bf16[512,1024]{1,0:T(8,128)(2,1)}, u32[]{:S(2)}) copy-start(bf16[512,1024]{1,0:T(8,128)(2,1)} %all-reduce.5.cloned.1.call-done) | copy-start | bytes 3145732
Sparse Core Ops, SparseCore 0:
  14.0 22.3 reduce-scatter.1
  41.7 55.5 all-reduce.4
  99.8 34.0 all-reduce.2
where the time goes:
time: 145 us; the launch traced here: 143 us
  waiting for transfers between devices  111 us (77%)
  between operations  13.3 us (9%)
  other arithmetic  8.07 us (6%)
  local copies, waits for them, and re-layouts  5.57 us (4%)
  matrix products  4.84 us (3%)
    psum x1, waiting for transfers between devices, select_pivots(): lax.psum(picked, ('shell', 'row')).astype(jnp.float32).astype(jnp.bfloat16)  53.2 us
    psum x1, waiting for transfers between devices, broadcast(): return lax.psum(block, axis)  35.2 us
    reduce_scatter x1, waiting for transfers between devices, reduce_tiles(): lax.psum_scatter(term_rows(jnp.int32(0), owned_rows * lax.axis_size('shel...  22.4 us
    gather x1, local copies, waits for them, and re-layouts, pick_rows(): jnp.take(matrix_rows, jnp.clip(local_index, 0, held_rows - 1), axis=0)  3.77 us
    neg x2, other arithmetic, complex_block(): lower_half = jnp.concatenate([-imag_part, real_part], axis=1)  3.27 us
  transfers between devices with their start and end apart: 3, of which 3 were waited for; matrix products, arithmetic and copies ran while one was open for 3% of the time, Pallas kernels for 0%

commit v1 on v0

v1 whole, which is shorter than its diff:
```python
import functools
import jax
import jax.numpy as jnp
from jax import lax
from jax.experimental import pallas as pl
from jax.experimental.pallas import tpu as pltpu
from jax.sharding import PartitionSpec as P

MESH = pl.DeviceIdType.MESH
CORES = 2


def kernel(shells, rows, cols, chunk, left_ref, right_ref, point_ref, shell_ref, green_ref, pivot_ref,
           inverse_ref, out_ref, weights, stacked, part, outgoing, incoming, coupling, owned, mult,
           select, y_send, y_recv, x_send, x_recv, f_send, f_recv, m_send, m_recv):
    s = lax.axis_index("shell")
    r = lax.axis_index("row")
    col = lax.axis_index("col")
    chips = rows // CORES
    h = r // CORES
    core = lax.rem(r, CORES)
    sibling = h * CORES + (CORES - 1 - core)
    points = right_ref.shape[1]
    width = right_ref.shape[2]
    tile_rows = left_ref.shape[1]
    own = tile_rows // shells
    pieces = own // chunk
    half = mult.shape[2]
    halves = chunk // half
    bf16, f32 = jnp.bfloat16, jnp.float32

    barrier = pltpu.get_barrier_semaphore()

    def greet(**where):
        pl.semaphore_signal(barrier, inc=1, device_id=where, device_id_type=MESH)

    for o in range(1, shells):
        greet(shell=lax.rem(s + o, shells))
    for d in range(1, chips):
        greet(row=lax.rem(h + d, chips) * CORES + core)
    greet(row=sibling)

    @pl.when(col > 0)
    def _():
        greet(col=col - 1)

    @pl.when(col < cols - 1)
    def _():
        greet(col=col + 1)

    count = green_ref.shape[0]
    index = shell_ref[...].reshape(1, points)
    point = point_ref[...].reshape(1, points)
    hot = jnp.where(lax.broadcasted_iota(jnp.int32, (count, points), 0) == index, point, 0.0)
    table = jnp.concatenate(
        [jnp.broadcast_to(green_ref[:, i : i + 1], (count, 128)) for i in range(2)], axis=1
    )
    weights[...] = lax.dot_general(
        hot, table, (((0,), (0,)), ((), ())), precision=lax.Precision.HIGHEST, preferred_element_type=f32
    )

    def weigh(i, carry):
        at = pl.ds(pl.multiple_of(i * 128, 128), 128)
        low = pl.ds(pl.multiple_of(points + i * 128, 128), 128)
        w_real = jnp.concatenate([weights[at, :128]] * (width // 128), axis=1)
        w_imag = jnp.concatenate([weights[at, 128:]] * (width // 128), axis=1)
        b_real = right_ref[0, at, :].astype(f32)
        b_imag = right_ref[1, at, :].astype(f32)
        real = (w_real * b_real - w_imag * b_imag).astype(bf16)
        imag = (w_real * b_imag + w_imag * b_real).astype(bf16)
        stacked[at, :width] = real
        stacked[at, width:] = imag
        stacked[low, :width] = -imag
        stacked[low, width:] = real
        return carry

    lax.fori_loop(0, points // 128, weigh, 0)

    def span(first, size):
        return pl.ds(pl.multiple_of(first, size), size)

    def y_copy(o, j, c, group):
        at = span(group * own + c * chunk, chunk)
        return pltpu.make_async_remote_copy(
            src_ref=outgoing.at[at], dst_ref=incoming.at[o - 1, at],
            send_sem=y_send.at[o - 1, j, c], recv_sem=y_recv.at[o - 1, j, c],
            device_id={"shell": lax.rem(s + o, shells)}, device_id_type=MESH,
        )

    def x_copy(d, j, c, group, row):
        at = span(row * tile_rows + group * own + c * chunk, chunk)
        return pltpu.make_async_remote_copy(
            src_ref=coupling.at[at], dst_ref=coupling.at[at],
            send_sem=x_send.at[d - 1, j, c], recv_sem=x_recv.at[d - 1, j, c],
            device_id={"row": lax.rem(h + d, chips) * CORES + core}, device_id_type=MESH,
        )

    def f_copy(d, j, c, group, row):
        at = span(row * tile_rows + group * own + c * chunk, chunk)
        return pltpu.make_async_remote_copy(
            src_ref=coupling.at[at], dst_ref=coupling.at[at],
            send_sem=f_send.at[d, j, c], recv_sem=f_recv.at[d, j, c],
            device_id={"row": sibling}, device_id_type=MESH,
        )

    def m_copy(i):
        return pltpu.make_async_remote_copy(
            src_ref=mult.at[i], dst_ref=mult.at[i], send_sem=m_send.at[i], recv_sem=m_recv.at[i],
            device_id={"col": col + 1}, device_id_type=MESH,
        )

    for k in range(shells):
        group = lax.rem(s + 1 + k, shells)
        at = span(group * own, own)
        left = jnp.concatenate([left_ref[0, at, :], left_ref[1, at, :]], axis=1)
        term = jnp.dot(left, stacked[...], preferred_element_type=f32)
        part[at, :] = term
        outgoing[at, :] = term.astype(bf16)
        if k == 0:
            line = jnp.minimum(col, 1) + jnp.minimum(cols - 1 - col, 1)
            pl.semaphore_wait(barrier, shells - 1 + chips + line)

        for c in range(pieces):
            for o in range(1, shells):
                y_copy(o, (1 + k - o) % shells, c, group).start()

    pivots = pivot_ref[...].reshape(1, -1)

    def choose(i, carry):
        at = span(i * 128, 128)
        line = lax.broadcasted_iota(jnp.int32, (128, pivots.shape[1]), 0) + i * 128
        select[at, :] = jnp.where(line == pivots, 1.0, 0.0).astype(bf16)
        return carry

    lax.fori_loop(0, select.shape[0] // 128, choose, 0)

    def take_y(j, c):
        group = lax.rem(s + j, shells)
        at = span(group * own + c * chunk, chunk)
        total = part[at, :]
        for o in range(1, shells):
            y_copy(o, j, c, group).wait_recv()
            total = total + incoming[o - 1, at, :].astype(f32)
        coupling[span(r * tile_rows + group * own + c * chunk, chunk), :] = total.astype(bf16)
        if j == 0:
            owned[c * chunk : (c + 1) * chunk, :] = total
        for d in range(1, chips):
            x_copy(d, j, c, group, r).start()
        f_copy(0, j, c, group, r).start()
        if j == 0:

            @pl.when(col == 0)
            def _():
                panel = owned[c * chunk : (c + 1) * chunk, :]
                high = panel.astype(bf16)
                low = (panel - high.astype(f32)).astype(bf16)
                four = jnp.concatenate(
                    [high[:, :width], low[:, :width], high[:, width:], low[:, width:]], axis=0
                )
                by_real = jnp.dot(four, inverse_ref[0], preferred_element_type=f32)
                by_imag = jnp.dot(four, inverse_ref[1], preferred_element_type=f32)

                def pick(product, first):
                    return product[first : first + chunk] + product[first + chunk : first + 2 * chunk]

                m_real = (pick(by_real, 0) - pick(by_imag, 2 * chunk)).astype(bf16)
                m_imag = (pick(by_imag, 0) + pick(by_real, 2 * chunk)).astype(bf16)
                for p in range(halves):
                    i = c * halves + p
                    mult[i, 0] = m_real[p * half : (p + 1) * half]
                    mult[i, 1] = m_imag[p * half : (p + 1) * half]
                    if cols > 1:
                        m_copy(i).start()

    def take_x(j, c):
        group = lax.rem(s + j, shells)
        for d in range(1, chips):
            row = lax.rem(h - d + chips, chips) * CORES + core
            x_copy(d, j, c, group, row).wait_recv()
            f_copy(d, j, c, group, row).start()

    def pass_mult(i):
        @pl.when((col > 0) & (col < cols - 1))
        def _():
            m_copy(i).wait_recv()
            m_copy(i).start()

    steps = [(j, c) for j in range(shells) for c in range(pieces)]
    passes = pieces * halves
    done = 0
    for n, (j, c) in enumerate(steps):
        take_y(j, c)
        if n >= 1:
            take_x(*steps[n - 1])
        if n >= len(steps) // 2 and done < passes:
            pass_mult(done)
            done += 1
    if done < passes:
        pass_mult(done)
        done += 1
    take_x(*steps[-1])
    while done < passes:
        pass_mult(done)
        done += 1

    for j, c in steps:
        group = lax.rem(s + j, shells)
        f_copy(0, j, c, group, sibling).wait_recv()
        for d in range(1, chips):
            row = lax.rem(h - d + chips, chips) * CORES + (CORES - 1 - core)
            f_copy(d, j, c, group, row).wait_recv()

    @pl.when((col == cols - 1) & (col > 0))
    def _():
        for i in range(passes):
            m_copy(i).wait_recv()

    factors = jnp.concatenate(
        [mult[i, p] for p in range(2) for i in range(passes)], axis=0
    )
    spread = lax.dot_general(
        factors, select[...], (((1,), (1,)), ((), ())), preferred_element_type=f32
    ).astype(bf16)
    product = jnp.dot(spread, coupling[...], preferred_element_type=f32)
    out_ref[0, 0, 0] = owned[:, :width] - (product[:own, :width] - product[own:, width:])
    out_ref[1, 0, 0] = owned[:, width:] - (product[:own, width:] + product[own:, :width])

    for j, c in steps:
        group = lax.rem(s + j, shells)
        for o in range(1, shells):
            y_copy(o, j, c, group).wait_send()
        f_copy(0, j, c, group, r).wait_send()
        for d in range(1, chips):
            x_copy(d, j, c, group, r).wait_send()
            f_copy(d, j, c, group, lax.rem(h - d + chips, chips) * CORES + core).wait_send()

    @pl.when(col < cols - 1)
    def _():
        for i in range(passes):
            m_copy(i).wait_send()


def body(sizes, left_basis, right_basis, point_weight, shell_index, green_table, pivot_rows, diag_inverse):
    shells, rows, cols = sizes
    chips = rows // CORES
    tile_rows, points = left_basis.shape[1:]
    width = right_basis.shape[2]
    own = tile_rows // shells
    chunk = own // 2
    half = chunk // 2
    pieces = own // chunk
    all_rows = rows * tile_rows
    bf16, f32 = jnp.bfloat16, jnp.float32
    vmem = pl.BlockSpec(memory_space=pltpu.VMEM)
    sems = pltpu.SemaphoreType.DMA
    return pl.pallas_call(
        functools.partial(kernel, shells, rows, cols, chunk),
        out_shape=jax.ShapeDtypeStruct((2, 1, 1, own, width), f32),
        in_specs=[vmem] * 7,
        out_specs=vmem,
        scratch_shapes=[
            pltpu.VMEM((points, 256), f32),
            pltpu.VMEM((2 * points, 2 * width), bf16),
            pltpu.VMEM((tile_rows, 2 * width), f32),
            pltpu.VMEM((tile_rows, 2 * width), bf16),
            pltpu.VMEM((max(shells - 1, 1), tile_rows, 2 * width), bf16),
            pltpu.VMEM((all_rows, 2 * width), bf16),
            pltpu.VMEM((own, 2 * width), f32),
            pltpu.VMEM((own // half, 2, half, width), bf16),
            pltpu.VMEM((all_rows, pivot_rows.shape[0]), bf16),
            sems((max(shells - 1, 1), shells, pieces)),
            sems((max(shells - 1, 1), shells, pieces)),
            sems((max(chips - 1, 1), shells, pieces)),
            sems((max(chips - 1, 1), shells, pieces)),
            sems((chips, shells, pieces)),
            sems((chips, shells, pieces)),
            sems((own // half,)),
            sems((own // half,)),
        ],
        compiler_params=pltpu.CompilerParams(
            collective_id=0, has_side_effects=True, vmem_limit_bytes=56 * 2**20
        ),
        cost_estimate=pl.CostEstimate(
            flops=2 * tile_rows * 2 * points * 2 * width + 4 * own * all_rows * 2 * width,
            bytes_accessed=8 * 2**20,
            transcendentals=0,
        ),
    )(left_basis, right_basis, point_weight, shell_index, green_table, pivot_rows, diag_inverse)


def solution(mesh):
    sizes = tuple(mesh.shape[name] for name in ("shell", "row", "col"))
    return jax.shard_map(
        functools.partial(body, sizes),
        mesh=mesh,
        in_specs=(
            P(None, "row", "shell"),
            P(None, "shell", "col"),
            P("shell"),
            P("shell"),
            P(),
            P(),
            P(),
        ),
        out_specs=P(None, "row", "shell", None, "col"),
        check_vma=False,
    )
```

time: 145 us -> 35.4 us (0.24)
  the two profiles are of different devices: /device:TPU:1 before, /device:TPU:24 now
where the time goes in v1:
time: 35.4 us; the launch traced here: 35.2 us
  Pallas kernels  32 us (90%)
  local copies, waits for them, and re-layouts  3.23 us (9%)
    pallas_call x1, Pallas kernels, body(): pl.pallas_call(functools.partial(kernel, shells, rows, cols, chunk), out_...  32 us
    unnamed x2, local copies, waits for them, and re-layouts  3.23 us

profile of v1, /device:TPU:24, one launch (start us, length us, event | category | flops | bytes accessed | tf_op | source)
XLA Modules:
  0.0 35.2 jit_solution(12027281520600985482)
XLA Ops:
  0.0 1.4 %copy.8.green_ref = f32[12,2]{1,0:T(8,128)} copy(f32[12,2]{0,1:T(2,128)} %param.11) | data formatting | bytes 192 | tf_op args[4]
  1.4 32.0 %shard_map.73 = f32[2,1,1,128,512]{4,3,2,1,0:T(8,128)} custom-call(bf16[2,256,768]{2,1,0:T(8,128)(2,1)} %left_ref.1, bf16[2,768,512]{2,1,0:T(8,128)(2,1)} %right_ref.1, f32[768]{0:T(1024)} %point_ref.1, s32[768]{0:T(1024)} %shell_ref.1, f32[12,2]{1,0:T(8,128)} %copy.8.green_ref, s32[512]{0:T(512)} %pivot_ref.1, bf16[2,512,512]{2,1,0:T(8,128)(2,1)} %inverse_ref.1), custom_call_target="tpu_custom_call" | custom-call | flops 1342177280 | bytes 8388608 | tf_op jit(solution)/shard_map/pallas_call | solution.py:256
  33.4 1.9 %copy.10 = f32[2,1,1,128,512]{4,3,2,1,0:T(8,128)} copy(f32[2,1,1,128,512]{4,3,2,1,0:T(8,128)} %shard_map.73) | data formatting | bytes 1048576

commit v2 on v1

--- a/solution.py
+++ b/solution.py
@@ -1,4 +1,5 @@
 import functools
+import math
 import jax
 import jax.numpy as jnp
 from jax import lax
@@ -10,9 +11,10 @@
 CORES = 2
 
 
-def kernel(shells, rows, cols, chunk, left_ref, right_ref, point_ref, shell_ref, green_ref, pivot_ref,
-           inverse_ref, out_ref, weights, stacked, part, outgoing, incoming, coupling, owned, mult,
-           select, y_send, y_recv, x_send, x_recv, f_send, f_recv, m_send, m_recv):
+def kernel(shells, rows, cols, chunk, left_hbm, right_hbm, point_hbm, shell_hbm, green_hbm, pivot_hbm,
+           inverse_hbm, out_ref, left_ref, right_ref, inverse_ref, point_ref, shell_ref, green_ref, pivot_ref, weights, weighted, product, part,
+           outgoing, incoming, coupling, owned, mult, select, spread, in_sem, y_send, y_recv, x_send,
+           x_recv, f_send, f_recv, m_send, m_recv):
     s = lax.axis_index("shell")
     r = lax.axis_index("row")
     col = lax.axis_index("col")
@@ -26,8 +28,37 @@
     own = tile_rows // shells
     pieces = own // chunk
     half = mult.shape[2]
-    halves = chunk // half
+    batch = 2 * chunk
+    halves = batch // half
     bf16, f32 = jnp.bfloat16, jnp.float32
+
+    slab = 256
+    slabs = points // slab
+    right_in = [
+        pltpu.make_async_copy(
+            right_hbm.at[:, pl.ds(b * slab, slab)], right_ref.at[:, pl.ds(b * slab, slab)], in_sem.at[b]
+        )
+        for b in range(slabs)
+    ]
+    left_in = pltpu.make_async_copy(left_hbm, left_ref, in_sem.at[slabs])
+    inverse_in = pltpu.make_async_copy(inverse_hbm, inverse_ref, in_sem.at[slabs + 1])
+    small_in = [
+        pltpu.make_async_copy(source, target, in_sem.at[slabs + 2 + i])
+        for i, (source, target) in enumerate([
+            (point_hbm, point_ref), (shell_hbm, shell_ref), (green_hbm, green_ref), (pivot_hbm, pivot_ref)
+        ])
+    ]
+    for copy in small_in[:3]:
+        copy.start()
+    right_in[0].start()
+    left_in.start()
+    for copy in right_in[1:]:
+        copy.start()
+    small_in[3].start()
+
+    @pl.when(col == 0)
+    def _():
+        inverse_in.start()
 
     barrier = pltpu.get_barrier_semaphore()
 
@@ -48,33 +79,30 @@
     def _():
         greet(col=col + 1)
 
-    count = green_ref.shape[0]
+    for copy in small_in[:3]:
+        copy.wait()
+    count = green_ref.shape[1]
     index = shell_ref[...].reshape(1, points)
     point = point_ref[...].reshape(1, points)
     hot = jnp.where(lax.broadcasted_iota(jnp.int32, (count, points), 0) == index, point, 0.0)
+    square = (count, count)
+    same = lax.broadcasted_iota(jnp.int32, square, 0) == lax.broadcasted_iota(jnp.int32, square, 1)
     table = jnp.concatenate(
-        [jnp.broadcast_to(green_ref[:, i : i + 1], (count, 128)) for i in range(2)], axis=1
+        [
+            jnp.broadcast_to(
+                jnp.sum(
+                    jnp.where(same, jnp.broadcast_to(green_ref[i : i + 1, :], square), 0.0),
+                    axis=1, keepdims=True,
+                ),
+                (count, 128),
+            )
+            for i in range(2)
+        ],
+        axis=1,
     )
     weights[...] = lax.dot_general(
         hot, table, (((0,), (0,)), ((), ())), precision=lax.Precision.HIGHEST, preferred_element_type=f32
     )
-
-    def weigh(i, carry):
-        at = pl.ds(pl.multiple_of(i * 128, 128), 128)
-        low = pl.ds(pl.multiple_of(points + i * 128, 128), 128)
-        w_real = jnp.concatenate([weights[at, :128]] * (width // 128), axis=1)
-        w_imag = jnp.concatenate([weights[at, 128:]] * (width // 128), axis=1)
-        b_real = right_ref[0, at, :].astype(f32)
-        b_imag = right_ref[1, at, :].astype(f32)
-        real = (w_real * b_real - w_imag * b_imag).astype(bf16)
-        imag = (w_real * b_imag + w_imag * b_real).astype(bf16)
-        stacked[at, :width] = real
-        stacked[at, width:] = imag
-        stacked[low, :width] = -imag
-        stacked[low, width:] = real
-        return carry
-
-    lax.fori_loop(0, points // 128, weigh, 0)
 
     def span(first, size):
         return pl.ds(pl.multiple_of(first, size), size)
@@ -109,13 +137,41 @@
             device_id={"col": col + 1}, device_id_type=MESH,
         )
 
+    def left_rows(group, at):
+        rows_at = span(group * own, own)
+        return jnp.concatenate([left_ref[0, rows_at, at], left_ref[1, rows_at, at]], axis=0)
+
+    def combine(four):
+        real = four[:own, :width] - four[own:, width:]
+        return real, four[:own, width:] + four[own:, :width]
+
+    first = lax.rem(s + 1, shells)
+    for b in range(slabs):
+        at = pl.ds(b * slab, slab)
+        right_in[b].wait()
+        w_real = jnp.concatenate([weights[at, :128]] * (width // 128), axis=1)
+        w_imag = jnp.concatenate([weights[at, 128:]] * (width // 128), axis=1)
+        b_real = right_ref[0, at, :].astype(f32)
+        b_imag = right_ref[1, at, :].astype(f32)
+        weighted[at, :width] = (w_real * b_real - w_imag * b_imag).astype(bf16)
+        weighted[at, width:] = (w_real * b_imag + w_imag * b_real).astype(bf16)
+        if b == 0:
+            left_in.wait()
+        term = jnp.dot(left_rows(first, at), weighted[at, :], preferred_element_type=f32)
+        product[...] = term if b == 0 else product[...] + term
+
     for k in range(shells):
         group = lax.rem(s + 1 + k, shells)
         at = span(group * own, own)
-        left = jnp.concatenate([left_ref[0, at, :], left_ref[1, at, :]], axis=1)
-        term = jnp.dot(left, stacked[...], preferred_element_type=f32)
-        part[at, :] = term
-        outgoing[at, :] = term.astype(bf16)
+        if k > 0:
+            product[...] = jnp.dot(
+                left_rows(group, pl.ds(0, points)), weighted[...], preferred_element_type=f32
+            )
+        real, imag = combine(product[...])
+        part[at, :width] = real
+        part[at, width:] = imag
+        outgoing[at, :width] = real.astype(bf16)
+        outgoing[at, width:] = imag.astype(bf16)
         if k == 0:
             line = jnp.minimum(col, 1) + jnp.minimum(cols - 1 - col, 1)
             pl.semaphore_wait(barrier, shells - 1 + chips + line)
@@ -124,6 +180,7 @@
             for o in range(1, shells):
                 y_copy(o, (1 + k - o) % shells, c, group).start()
 
+    small_in[3].wait()
     pivots = pivot_ref[...].reshape(1, -1)
 
     def choose(i, carry):
@@ -147,11 +204,14 @@
         for d in range(1, chips):
             x_copy(d, j, c, group, r).start()
         f_copy(0, j, c, group, r).start()
-        if j == 0:
+        if j == 0 and (c + 1) * chunk % batch == 0:
 
             @pl.when(col == 0)
             def _():
-                panel = owned[c * chunk : (c + 1) * chunk, :]
+                base = (c + 1) * chunk - batch
+                if base == 0:
+                    inverse_in.wait()
+                panel = owned[base : base + batch, :]
                 high = panel.astype(bf16)
                 low = (panel - high.astype(f32)).astype(bf16)
                 four = jnp.concatenate(
@@ -160,13 +220,13 @@
                 by_real = jnp.dot(four, inverse_ref[0], preferred_element_type=f32)
                 by_imag = jnp.dot(four, inverse_ref[1], preferred_element_type=f32)
 
-                def pick(product, first):
-                    return product[first : first + chunk] + product[first + chunk : first + 2 * chunk]
-
-                m_real = (pick(by_real, 0) - pick(by_imag, 2 * chunk)).astype(bf16)
-                m_imag = (pick(by_imag, 0) + pick(by_real, 2 * chunk)).astype(bf16)
+                def pick(value, at):
+                    return value[at : at + batch] + value[at + batch : at + 2 * batch]
+
+                m_real = (pick(by_real, 0) - pick(by_imag, 2 * batch)).astype(bf16)
+                m_imag = (pick(by_imag, 0) + pick(by_real, 2 * batch)).astype(bf16)
                 for p in range(halves):
-                    i = c * halves + p
+                    i = base // half + p
                     mult[i, 0] = m_real[p * half : (p + 1) * half]
                     mult[i, 1] = m_imag[p * half : (p + 1) * half]
                     if cols > 1:
@@ -185,45 +245,54 @@
             m_copy(i).wait_recv()
             m_copy(i).start()
 
+    def take_sibling(d, j, c):
+        group = lax.rem(s + j, shells)
+        row = lax.rem(h - d + chips, chips) * CORES + (CORES - 1 - core)
+        f_copy(d, j, c, group, row).wait_recv()
+
     steps = [(j, c) for j in range(shells) for c in range(pieces)]
-    passes = pieces * halves
+    passes = own // half
     done = 0
     for n, (j, c) in enumerate(steps):
         take_y(j, c)
-        if n >= 1:
-            take_x(*steps[n - 1])
-        if n >= len(steps) // 2 and done < passes:
+        if n >= pieces - 1 and done < passes:
             pass_mult(done)
             done += 1
-    if done < passes:
-        pass_mult(done)
-        done += 1
-    take_x(*steps[-1])
-    while done < passes:
-        pass_mult(done)
-        done += 1
-
-    for j, c in steps:
-        group = lax.rem(s + j, shells)
-        f_copy(0, j, c, group, sibling).wait_recv()
-        for d in range(1, chips):
-            row = lax.rem(h - d + chips, chips) * CORES + (CORES - 1 - core)
-            f_copy(d, j, c, group, row).wait_recv()
+        if n >= 2:
+            take_x(*steps[n - 2])
+    for i in range(done, passes):
+        pass_mult(i)
+    take_x(*steps[-2])
 
     @pl.when((col == cols - 1) & (col > 0))
     def _():
         for i in range(passes):
             m_copy(i).wait_recv()
 
-    factors = jnp.concatenate(
-        [mult[i, p] for p in range(2) for i in range(passes)], axis=0
-    )
-    spread = lax.dot_general(
+    factors = jnp.concatenate([mult[i, p] for p in range(2) for i in range(passes)], axis=0)
+    spread[...] = lax.dot_general(
         factors, select[...], (((1,), (1,)), ((), ())), preferred_element_type=f32
     ).astype(bf16)
-    product = jnp.dot(spread, coupling[...], preferred_element_type=f32)
-    out_ref[0, 0, 0] = owned[:, :width] - (product[:own, :width] - product[own:, width:])
-    out_ref[1, 0, 0] = owned[:, width:] - (product[:own, width:] + product[own:, :width])
+    for j, c in steps:
+        take_sibling(0, j, c)
+    near = span(h * CORES * tile_rows, CORES * tile_rows)
+    product[...] = jnp.dot(spread[:, near], coupling[near, :], preferred_element_type=f32)
+    take_x(*steps[-1])
+    for j in range(shells):
+        group = lax.rem(s + j, shells)
+        for d in range(1, chips):
+            for c in range(pieces):
+                take_sibling(d, j, c)
+            first_row = lax.rem(h - d + chips, chips) * CORES * tile_rows + group * own
+            spots = [span(first_row + i * tile_rows, own) for i in range(CORES)]
+            product[...] += jnp.dot(
+                jnp.concatenate([spread[:, at] for at in spots], axis=1),
+                jnp.concatenate([coupling[at, :] for at in spots], axis=0),
+                preferred_element_type=f32,
+            )
+    real, imag = combine(product[...])
+    out_ref[0, 0, 0] = owned[:, :width] - real
+    out_ref[1, 0, 0] = owned[:, width:] - imag
 
     for j, c in steps:
         group = lax.rem(s + j, shells)
@@ -246,28 +315,41 @@
     tile_rows, points = left_basis.shape[1:]
     width = right_basis.shape[2]
     own = tile_rows // shells
-    chunk = own // 2
-    half = chunk // 2
+    chunk = own // 4
+    half = chunk
     pieces = own // chunk
     all_rows = rows * tile_rows
     bf16, f32 = jnp.bfloat16, jnp.float32
     vmem = pl.BlockSpec(memory_space=pltpu.VMEM)
     sems = pltpu.SemaphoreType.DMA
+    buffers = [
+        ((2, tile_rows, points), bf16),
+        ((2, points, width), bf16),
+        (diag_inverse.shape, bf16),
+        (point_weight.shape, f32),
+        (shell_index.shape, jnp.int32),
+        (green_table.shape[::-1], f32),
+        (pivot_rows.shape, jnp.int32),
+        ((points, 256), f32),
+        ((points, 2 * width), bf16),
+        ((2 * own, 2 * width), f32),
+        ((tile_rows, 2 * width), f32),
+        ((tile_rows, 2 * width), bf16),
+        ((max(shells - 1, 1), tile_rows, 2 * width), bf16),
+        ((all_rows, 2 * width), bf16),
+        ((own, 2 * width), f32),
+        ((own // half, 2, half, width), bf16),
+        ((all_rows, pivot_rows.shape[0]), bf16),
+        ((2 * own, all_rows), bf16),
+    ]
+    held = sum(math.prod(shape) * jnp.dtype(kind).itemsize for shape, kind in buffers)
     return pl.pallas_call(
         functools.partial(kernel, shells, rows, cols, chunk),
         out_shape=jax.ShapeDtypeStruct((2, 1, 1, own, width), f32),
-        in_specs=[vmem] * 7,
+        in_specs=[pl.BlockSpec(memory_space=pltpu.HBM)] * 7,
         out_specs=vmem,
-        scratch_shapes=[
-            pltpu.VMEM((points, 256), f32),
-            pltpu.VMEM((2 * points, 2 * width), bf16),
-            pltpu.VMEM((tile_rows, 2 * width), f32),
-            pltpu.VMEM((tile_rows, 2 * width), bf16),
-            pltpu.VMEM((max(shells - 1, 1), tile_rows, 2 * width), bf16),
-            pltpu.VMEM((all_rows, 2 * width), bf16),
-            pltpu.VMEM((own, 2 * width), f32),
-            pltpu.VMEM((own // half, 2, half, width), bf16),
-            pltpu.VMEM((all_rows, pivot_rows.shape[0]), bf16),
+        scratch_shapes=[pltpu.VMEM(shape, kind) for shape, kind in buffers] + [
+            sems((points // 256 + 6,)),
             sems((max(shells - 1, 1), shells, pieces)),
             sems((max(shells - 1, 1), shells, pieces)),
             sems((max(chips - 1, 1), shells, pieces)),
@@ -285,7 +367,7 @@
             bytes_accessed=8 * 2**20,
             transcendentals=0,
         ),
-    )(left_basis, right_basis, point_weight, shell_index, green_table, pivot_rows, diag_inverse)
+    )(left_basis, right_basis, point_weight, shell_index, green_table.T, pivot_rows, diag_inverse)
 
 
 def solution(mesh):

time: 35.4 us -> 28.3 us (0.80)
  the two profiles are of different devices: /device:TPU:24 before, /device:TPU:17 now
where the time goes in v2:
time: 28.3 us; the launch traced here: 28.1 us
  Pallas kernels  26.2 us (93%)
  local copies, waits for them, and re-layouts  1.87 us (7%)
    pallas_call x1, Pallas kernels, body(): pl.pallas_call(functools.partial(kernel, shells, rows, cols, chunk), out_...  26.2 us
    unnamed x1, local copies, waits for them, and re-layouts  1.87 us

profile of v2, /device:TPU:17, one launch (start us, length us, event | category | flops | bytes accessed | tf_op | source)
XLA Modules:
  0.0 28.1 jit_solution(3845526037555454524)
XLA Ops:
  0.0 26.2 %shard_map.73 = f32[2,1,1,128,512]{4,3,2,1,0:T(8,128)} custom-call(bf16[2,256,768]{2,1,0:T(8,128)(2,1)} %left_hbm.1, bf16[2,768,512]{2,1,0:T(8,128)(2,1)} %right_hbm.1, f32[768]{0:T(1024)} %point_hbm.1, s32[768]{0:T(1024)} %shell_hbm.1, f32[2,12]{1,0:T(2,128)} %bitcast.1, s32[512]{0:T(512)} %pivot_hbm.1, bf16[2,512,512]{2,1,0:T(8,128)(2,1)} %inverse_hbm.1), custom_call_target="tpu_custom_call" | custom-call | flops 1342177280 | bytes 8388608 | tf_op jit(solution)/shard_map/pallas_call | solution.py:346
  26.2 1.9 %copy.9 = f32[2,1,1,128,512]{4,3,2,1,0:T(8,128)} copy(f32[2,1,1,128,512]{4,3,2,1,0:T(8,128)} %shard_map.73) | data formatting | bytes 1048576

commit v3 on v2

--- a/solution.py
+++ b/solution.py
@@ -82,10 +82,17 @@
     for copy in small_in[:3]:
         copy.wait()
     count = green_ref.shape[1]
+    padded = -(-count // 16) * 16
     index = shell_ref[...].reshape(1, points)
-    point = point_ref[...].reshape(1, points)
-    hot = jnp.where(lax.broadcasted_iota(jnp.int32, (count, points), 0) == index, point, 0.0)
-    square = (count, count)
+    match = lax.broadcasted_iota(jnp.int32, (padded, points), 0) == index
+
+    def pieces_of(value):
+        first = value.astype(bf16).astype(f32)
+        second = (value - first).astype(bf16).astype(f32)
+        return first, second, value - first - second
+
+    hot = [jnp.where(match, piece, 0.0).astype(bf16) for piece in pieces_of(point_ref[...].reshape(1, points))]
+    square = (padded, count)
     same = lax.broadcasted_iota(jnp.int32, square, 0) == lax.broadcasted_iota(jnp.int32, square, 1)
     table = jnp.concatenate(
         [
@@ -94,14 +101,19 @@
                     jnp.where(same, jnp.broadcast_to(green_ref[i : i + 1, :], square), 0.0),
                     axis=1, keepdims=True,
                 ),
-                (count, 128),
+                (padded, 128),
             )
             for i in range(2)
         ],
         axis=1,
     )
+    green = [piece.astype(bf16) for piece in pieces_of(table)]
+    pairs = [(i, j) for i in range(3) for j in range(3 - i)]
     weights[...] = lax.dot_general(
-        hot, table, (((0,), (0,)), ((), ())), precision=lax.Precision.HIGHEST, preferred_element_type=f32
+        jnp.concatenate([hot[i] for i, _ in pairs], axis=0),
+        jnp.concatenate([green[j] for _, j in pairs], axis=0),
+        (((0,), (0,)), ((), ())),
+        preferred_element_type=f32,
     )
 
     def span(first, size):
@@ -345,7 +357,7 @@
     held = sum(math.prod(shape) * jnp.dtype(kind).itemsize for shape, kind in buffers)
     return pl.pallas_call(
         functools.partial(kernel, shells, rows, cols, chunk),
-        out_shape=jax.ShapeDtypeStruct((2, 1, 1, own, width), f32),
+        out_shape=pltpu.VMEM((2, 1, 1, own, width), f32),
         in_specs=[pl.BlockSpec(memory_space=pltpu.HBM)] * 7,
         out_specs=vmem,
         scratch_shapes=[pltpu.VMEM(shape, kind) for shape, kind in buffers] + [

time: 28.3 us -> 25.2 us (0.89)
  Pallas kernels: 26.2 us -> 24.2 us
  local copies, waits for them, and re-layouts: 1.87 us -> 0.8 us
    pallas_call x1, Pallas kernels: 26.2 us -> 24.2 us  [body(): pl.pallas_call(functools.partial(kernel, shells, rows, cols, chunk), out_...]
    unnamed x1, local copies, waits for them, and re-layouts: 1.87 us -> 0.8 us
where the time goes in v3:
time: 25.2 us; the launch traced here: 25 us
  Pallas kernels  24.2 us (96%)
  local copies, waits for them, and re-layouts  0.8 us (3%)
    pallas_call x1, Pallas kernels, body(): pl.pallas_call(functools.partial(kernel, shells, rows, cols, chunk), out_...  24.2 us
    unnamed x1, local copies, waits for them, and re-layouts  0.8 us

profile of v3, /device:TPU:17, one launch (start us, length us, event | category | flops | bytes accessed | tf_op | source)
XLA Modules:
  0.0 25.0 jit_solution(14699653278900660692)
XLA Ops:
  0.0 24.2 %shard_map.73 = f32[2,1,1,128,512]{4,3,2,1,0:T(8,128)S(1)} custom-call(bf16[2,256,768]{2,1,0:T(8,128)(2,1)} %left_hbm.1, bf16[2,768,512]{2,1,0:T(8,128)(2,1)} %right_hbm.1, f32[768]{0:T(1024)} %point_hbm.1, s32[768]{0:T(1024)} %shell_hbm.1, f32[2,12]{1,0:T(2,128)} %bitcast.1, s32[512]{0:T(512)} %pivot_hbm.1, bf16[2,512,512]{2,1,0:T(8,128)(2,1)} %inverse_hbm.1), custom_call_target="tpu_custom_call" | custom-call | flops 1342177280 | bytes 8388608 | tf_op jit(solution)/shard_map/pallas_call | solution.py:358
  24.2 0.8 %copy.9 = f32[2,1,1,128,512]{4,3,2,1,0:T(8,128)} copy(f32[2,1,1,128,512]{4,3,2,1,0:T(8,128)S(1)} %shard_map.73) | data formatting | bytes 1048576
